TPU v7x, 512 devices: a whole 4x4x16 slice. The times are simulated.
512 devices in a mesh: ctx: 64 (over z_hi, x, y), tp: 8 (over z_lo, core).
Axes of the slice: x: 4, y: 4, z: 16 (z_hi: 4, z_lo: 4; z = z_hi * 4 + z_lo), core: 2. Of those that a mesh axis runs over, the one named last changes fastest.
Arguments:
- q_nope: bfloat16 [4096, 8192], P('ctx', 'tp'), may hold values from -4 to 4
- q_rope: bfloat16 [4096, 4096], P('ctx', 'tp'), may hold values from -4 to 4
- kv_cache: bfloat16 [4096, 576], P('ctx'), may hold values from -4 to 4
- w_uk: bfloat16 [64, 128, 512], P('tp'), may hold values from -0.5 to 0.5
- w_uv: bfloat16 [64, 512, 128], P('tp'), may hold values from -0.25 to 0.25
- w_out: bfloat16 [8192, 3584], P('tp', 'ctx'), may hold values from -1 to 1
- group_order: int32 [128], replicated, may hold values from 0 to 127, each once
- block_mask: int32 [128, 128], replicated, may hold values from 0 to 1, as said below
Outputs:
- mixed: bfloat16 [4096, 3584], P('ctx', 'tp')
Inputs may be any that keep to these rules, and one draw needn't show every extreme that they name: `group_order`: a permutation of 0 to 127. block_mask[i, i] is 1 and block_mask[i, j] is 0 for j > i.
All inputs are finite; a program needn't handle non-finite values.
Results may differ from a plain program's by a relative error of at most 0.019.
Values may be sent and summed in bfloat16 or wider, within the bound.
A program may use at most 64 MiB of HBM per device.

v0:
```python
import jax
import jax.numpy as jnp
from jax import lax
from jax.sharding import PartitionSpec as P


def on_device(q_nope, q_rope, kv_cache, w_uk, w_uv, w_out, group_order, block_mask):
    rows_here = q_nope.shape[0]
    group_count = group_order.shape[0]
    group_len = rows_here * lax.axis_size("ctx") // group_count
    heads_here = w_uk.shape[0]
    nope_dim = w_uk.shape[1]
    latent_dim = w_uk.shape[2]
    rope_dim = q_rope.shape[1] // heads_here
    value_dim = w_uv.shape[2]
    score_scale = (nope_dim + rope_dim) ** (-0.5)
    group_ids = jnp.arange(group_count, dtype=jnp.int32)

    def group_of(row_ids):
        matches = (row_ids // group_len)[:, None] == group_ids[None, :]
        return jnp.sum(jnp.where(matches, group_order[None, :], 0), axis=1)

    local_rows = lax.axis_index("ctx") * rows_here + jnp.arange(rows_here, dtype=jnp.int32)
    q_group = group_of(local_rows)
    q_pos = q_group * group_len + local_rows % group_len
    q_onehot = (q_group[:, None] == group_ids[None, :]).astype(jnp.float32)
    q_mask = jnp.dot(q_onehot, block_mask.astype(jnp.float32), preferred_element_type=jnp.float32)
    absorbed = jnp.einsum(
        "thn,hnc->thc",
        q_nope.reshape(rows_here, heads_here, nope_dim),
        w_uk,
        preferred_element_type=jnp.float32,
    ).astype(jnp.bfloat16)
    queries = jnp.concatenate([absorbed, q_rope.reshape(rows_here, heads_here, rope_dim)], axis=2)
    queries = jnp.transpose(queries, (1, 0, 2)).reshape(
        heads_here * rows_here, latent_dim + rope_dim
    )
    key_rows = lax.all_gather(kv_cache, "ctx", axis=0, tiled=True)
    key_start = jnp.int32(0)
    weighted = jnp.zeros((heads_here * rows_here, latent_dim), jnp.float32)
    totals = jnp.zeros((heads_here * rows_here,), jnp.float32)
    for offset in range(0, key_rows.shape[0], 1024):
        key_block = key_rows[offset : offset + 1024]
        block_len = key_block.shape[0]
        key_ids = key_start + offset + jnp.arange(block_len, dtype=jnp.int32)
        k_group = group_of(key_ids)
        k_pos = k_group * group_len + key_ids % group_len
        k_onehot = (k_group[:, None] == group_ids[None, :]).astype(jnp.float32)
        permitted = lax.dot_general(
            q_mask, k_onehot, (((1,), (1,)), ((), ())), preferred_element_type=jnp.float32
        )
        allowed = (permitted > 0.5) & (k_pos[None, :] <= q_pos[:, None])
        allowed = jnp.tile(allowed, (heads_here, 1))
        scores = (
            lax.dot_general(
                queries, key_block, (((1,), (1,)), ((), ())), preferred_element_type=jnp.float32
            )
            * score_scale
        )
        weights = jnp.where(allowed, jnp.exp(scores), 0.0)
        added = jnp.dot(
            weights.astype(jnp.bfloat16),
            key_block[:, :latent_dim],
            preferred_element_type=jnp.float32,
        )
        weighted, totals = (weighted + added, totals + jnp.sum(weights, axis=1))
    weighted, totals = (weighted, totals)
    latent_out = (
        (weighted / totals[:, None]).astype(jnp.bfloat16).reshape(heads_here, rows_here, latent_dim)
    )
    head_out = jnp.einsum(
        "htc,hcv->thv", latent_out, w_uv, preferred_element_type=jnp.float32
    ).astype(jnp.bfloat16)
    head_out = head_out.reshape(rows_here, heads_here * value_dim)
    partials = jnp.dot(
        head_out,
        lax.all_gather(w_out, "ctx", axis=1, tiled=True),
        preferred_element_type=jnp.float32,
    )
    return lax.psum_scatter(partials.astype(jnp.bfloat16), "tp", scatter_dimension=1, tiled=True)


def solution(mesh):
    in_specs = (
        P("ctx", "tp"),
        P("ctx", "tp"),
        P("ctx", None),
        P("tp", None, None),
        P("tp", None, None),
        P("tp", "ctx"),
        P(),
        P(),
    )
    out_specs = P("ctx", "tp")
    return jax.shard_map(
        on_device, mesh=mesh, in_specs=in_specs, out_specs=out_specs, check_vma=False
    )
```

profile of v0, /device:TPU:1, one launch (start us, length us, event | category | flops | bytes accessed | tf_op | source)
XLA Modules:
  0.0 400.8 jit_solution(9491852716935393731)
XLA Ops:
  6.5 0.0 copy-start
  6.5 0.0 copy-start.4
  6.5 0.0 copy-start.3
  6.5 0.0 all-gather.3.cloned.1.call-start
  6.5 0.7 all-gather.3.cloned.1.call-update
  7.3 0.0 all-gather.5.cloned.1.call-start
  7.3 0.7 all-gather.5.cloned.1.call-update
  8.0 0.0 reduce-scatter.4.cloned.1.call-start
  8.1 1.0 reshape.225
  9.1 0.8 select_reduce_fusion.4
  10.0 0.0 copy-done
  10.0 1.2 fusion.18
  11.2 0.1 pad_maximum_fusion
  11.3 0.0 copy-done.4
  11.3 1.4 select_reduce_fusion
  12.8 0.0 copy-done.3
  12.8 0.2 fusion.37
  12.9 0.4 fusion.22
  13.3 0.4 fusion.21
  13.7 0.4 fusion.23
  14.0 0.4 fusion.20
  14.4 154.3 %all-gather.3.cloned.1.call-done = bf16[4096,576]{1,0:T(8,128)(2,1)} async-done(((bf16[64,576]{1,0:T(8,128)(2,1)}), bf16[4096,576]{1,0:T(8,128)(2,1)}) %all-gather.3.cloned.1.call-update) | async-done | bytes 4718608 | tf_op jit(solution)/shard_map/all_gather | solution.py:38
  168.7 0.0 copy-start.1
  168.7 2.7 fusion.4
  171.4 2.6 fusion.2
  173.9 0.0 copy-done.1
  173.9 1.2 fusion.6
  175.2 1.2 fusion
  176.4 0.7 fusion.27
  177.2 0.7 convolution_add_fusion.2
  177.9 0.7 convolution_add_fusion.1
  178.6 0.0 copy-start.2
  178.6 0.7 fusion.17
  179.3 0.5 copy-done.2
  179.8 0.3 fusion.19
  180.1 170.2 %all-gather.5.cloned.1.call-done = bf16[1024,3584]{0,1:T(8,128)(2,1)} async-done(((bf16[1024,56]{0,1:T(8,128)(2,1)}), bf16[1024,3584]{0,1:T(8,128)(2,1)}) %all-gather.5.cloned.1.call-update) | async-done | bytes 7340048 | tf_op jit(solution)/shard_map/all_gather | solution.py:77
  350.3 5.4 %convolution_convert_fusion = bf16[64,3584]{1,0:T(8,128)(2,1)S(1)} fusion(bf16[1024,3584]{0,1:T(8,128)(2,1)} %all-gather.5.cloned.1.call-done, bf16[8,8,8,128]{3,2,1,0:T(8,128)(2,1)S(1)} %fusion.19), kind=kOutput, calls=%fused_computation | convolution fusion | flops 469991424 | bytes 7929856 | tf_op jit(solution)/shard_map/dot_general | solution.py:75
  355.8 1.2 copy.19
  357.0 0.0 reduce-scatter.4.cloned.1.call-update
  357.0 35.6 %reduce-scatter.4.cloned.1.call-done = bf16[448,64]{1,0:T(8,128)(2,1)} async-done(((bf16[3584,64]{1,0:T(8,128)(2,1)}), bf16[448,64]{1,0:T(8,128)(2,1)}) %reduce-scatter.4.cloned.1.call-update) | async-done | bytes 57360
  392.6 1.6 copy.20
  (10 shorter events, 0.1 us)
Async XLA Ops:
  6.5 3.4 copy-start
  6.5 4.7 %copy-start.4 = (s32[128]{0:T(128)S(1)}, s32[128]{0:T(128)}, u32[]{:S(2)}) copy-start(s32[128]{0:T(128)} %param.14) | copy-start | bytes 1540
  6.5 6.2 %copy-start.3 = (s32[128,128]{1,0:T(8,128)S(1)}, s32[128,128]{1,0:T(8,128)}, u32[]{:S(2)}) copy-start(s32[128,128]{1,0:T(8,128)} %param.15) | copy-start | bytes 196612
  6.5 162.1 %all-gather.3.cloned.1.call-start = ((), (), s32[]{:S(2)}) async-start(), calls=%async_computation.1 | async-start | bytes 5324800 | tf_op jit(solution)/shard_map/all_gather | solution.py:38
  7.3 343.1 %all-gather.5.cloned.1.call-start = ((), (), s32[]{:S(2)}) async-start(), calls=%async_computation.2 | async-start | bytes 7454720 | tf_op jit(solution)/shard_map/all_gather | solution.py:77
  8.0 384.6 %reduce-scatter.4.cloned.1.call-start = ((), (), s32[]{:S(2)}) async-start(), calls=%async_computation.3 | async-start | bytes 1032192
  168.7 5.3 %copy-start.1 = (bf16[4096,576]{1,0:T(8,128)(2,1)S(1)}, bf16[4096,576]{1,0:T(8,128)(2,1)}, u32[]{:S(2)}) copy-start(bf16[4096,576]{1,0:T(8,128)(2,1)} %all-gather.3.cloned.1.call-done) | copy-start | bytes 14155780
  178.6 1.2 copy-start.2
Sparse Core Ops, SparseCore 0:
  11.5 157.0 all-gather.2
  172.9 177.4 all-gather.4
  357.2 35.4 reduce-scatter.3
where the time goes:
time: 403 us; the launch traced here: 401 us
  waiting for transfers between devices  361 us (90%)
  matrix products  19.2 us (5%)
  between operations  13.3 us (3%)
  local copies, waits for them, and re-layouts  4.38 us (1%)
    all_gather x1, waiting for transfers between devices, on_device(): lax.all_gather(w_out, 'ctx', axis=1, tiled=True)  170 us
    all_gather x1, waiting for transfers between devices, on_device(): key_rows = lax.all_gather(kv_cache, 'ctx', axis=0, tiled=True)  154 us
    unnamed x4, waiting for transfers between devices  37 us
  transfers between devices with their start and end apart: 3, of which 3 were waited for; matrix products, arithmetic and copies ran while one was open for 4% of the time, Pallas kernels for 0%

commit v1 on v0

v1 whole, which is shorter than its diff:
```python
import jax
import jax.numpy as jnp
from jax import lax
from jax.experimental import pallas as pl
from jax.experimental.pallas import tpu as pltpu
from jax.sharding import PartitionSpec as P

MESH = pl.DeviceIdType.MESH
NT = (((1,), (1,)), ((), ()))
NN = (((1,), (0,)), ((), ()))
F32, BF16, I32 = jnp.float32, jnp.bfloat16, jnp.int32
MASKED = -1e30
N_SEMS = 128


def dot(a, b, dims=NN):
    return lax.dot_general(a, b, dims, preferred_element_type=F32)


def kernel(q_nope, q_rope, kv, w_uk_hbm, w_uv_hbm, w_out, order, mask, out,
           K, W, Q, acc, lanes, bias, w_uk, w_uv, H, XS, XR, S, R, A, send, recv, local):
    heads, nope, latent = w_uk.shape
    rope = q_rope.shape[1] // heads
    half = q_nope.shape[0] // 2
    rows = heads * half
    cols = w_out.shape[1]
    keys = 8 * half
    scale = (nope + rope) ** -0.5 * 1.4426950408889634

    c, t = lax.axis_index("ctx"), lax.axis_index("tp")
    z, x, y = c // 16, (c // 4) % 4, c % 4
    zl, core = t // 2, t % 2
    other = 1 - core

    def dev(dz=0, dx=0, dy=0, dl=0, k=core):
        cc = ((z + dz) % 4) * 16 + ((x + dx) % 4) * 4 + (y + dy) % 4
        return (cc, ((zl + dl) % 4) * 2 + k)

    sibling = dev(k=other)
    pending, used = [], [0]

    def push(src, dst, to):
        i = used[0]
        used[0] += 1
        d = pltpu.make_async_remote_copy(src, dst, send.at[i], recv.at[i], device_id=to, device_id_type=MESH)
        d.start()
        pending.append(d)
        return d

    loads = [pltpu.make_async_copy(w_uk_hbm, w_uk, local.at[0]), pltpu.make_async_copy(w_uv_hbm, w_uv, local.at[1])]
    for d in loads:
        d.start()

    K[0, 0, pl.ds(core, 1), 0] = kv[pl.ds(pl.multiple_of(core * half, half), half), :][None]

    barrier = pltpu.get_barrier_semaphore()
    partners = [dev(dz=1), dev(dz=3), dev(dx=1), dev(dx=3), sibling]
    partners += [dev(dl=dl, dy=dy) for dl in range(4) for dy in range(4) if dl or dy]
    for p in partners:
        pl.semaphore_signal(barrier, inc=1, device_id=p, device_id_type=MESH)
    pl.semaphore_wait(barrier, len(partners))

    lo, hi = pl.ds(0, half // 2), pl.ds(half // 2, half // 2)

    def kz_send():
        a = K.at[0, 0, core, 0]
        return push(a, K.at[3, 0, core, 0], dev(dz=1)), push(a, K.at[1, 0, core, 0], dev(dz=3))

    def kz_relay():
        return (push(K.at[3, 0, core, 0, lo], K.at[2, 0, core, 0, lo], dev(dz=1)),
                push(K.at[1, 0, core, 0, hi], K.at[2, 0, core, 0, hi], dev(dz=3)))

    def kx_send(dz):
        a = K.at[dz, 0, core, 0]
        return push(a, K.at[dz, 0, core, 3], dev(dx=1)), push(a, K.at[dz, 0, core, 1], dev(dx=3))

    def kx_relay(dz):
        return (push(K.at[dz, 0, core, 3, lo], K.at[dz, 0, core, 2, lo], dev(dx=1)),
                push(K.at[dz, 0, core, 1, hi], K.at[dz, 0, core, 2, hi], dev(dx=3)))

    def ky_send(dz):
        a = K.at[dz, 0, core]
        return push(a, K.at[dz, 3, core], dev(dy=1)), push(a, K.at[dz, 1, core], dev(dy=3))

    def ky_relay(dz):
        l, h = pl.ds(0, 2), pl.ds(2, 2)
        return (push(K.at[dz, 3, core, l], K.at[dz, 2, core, l], dev(dy=1)),
                push(K.at[dz, 1, core, h], K.at[dz, 2, core, h], dev(dy=3)))

    def share(dz, dy):
        return push(K.at[dz, dy, core], K.at[dz, dy, core], sibling)

    def arrived(ds):
        for d in ds:
            d.wait_recv()

    own_w = W.at[z, x]
    wl, wh = pl.ds(0, 32), pl.ds(32, 32)

    def wz_send():
        return push(own_w, own_w, dev(dz=1)), push(own_w, own_w, dev(dz=3))

    def wz_relay():
        a, b = W.at[(z + 3) % 4, x, wl], W.at[(z + 1) % 4, x, wh]
        return push(a, a, dev(dz=1)), push(b, b, dev(dz=3))

    def wx_send(dz):
        a = W.at[(z + dz) % 4, x]
        return push(a, a, dev(dx=1)), push(a, a, dev(dx=3))

    def wx_relay(dz):
        zz = (z + dz) % 4
        a, b = W.at[zz, (x + 3) % 4, wl], W.at[zz, (x + 1) % 4, wh]
        return push(a, a, dev(dx=1)), push(b, b, dev(dx=3))

    def attend(dz, dy, first=False):
        kc = K[dz, dy].reshape(keys, latent + rope)
        at = (dz * 4 + dy) * keys
        for i in range(2):
            r = pl.ds(i * rows, rows)
            s = dot(Q[r, :], kc, NT) * scale + bias[i : i + 1, at : at + keys]
            if first:
                key = lax.broadcasted_iota(I32, (rows, keys), 1) - i * keys // 2
                row = lax.broadcasted_iota(I32, (rows, keys), 0) % half
                s = jnp.where((key >= 0) & (key < half) & (key > row), MASKED, s)
            w = jnp.exp2(s)
            part = w[:, :128]
            for j in range(128, keys, 128):
                part = part + w[:, j : j + 128]
            added = dot(w.astype(BF16), kc[:, :latent])
            if first:
                lanes[r, :] = part
                acc[r, :] = added
            else:
                lanes[r, :] += part
                acc[r, :] += added

    kz = kz_send()
    kx = {0: kx_send(0)}

    eye = (lax.broadcasted_iota(I32, (64, cols), 0) == lax.broadcasted_iota(I32, (64, cols), 1)).astype(BF16)
    W[pl.ds(z, 1), pl.ds(x, 1)] = dot(eye, w_out[...], NT).astype(BF16)[None, None]
    wz = wz_send()

    groups = order.shape[1]
    named = (lax.broadcasted_iota(I32, (groups, groups), 0) == order[...]).astype(BF16)
    mine = (lax.broadcasted_iota(I32, (8, groups), 1) == 2 * c + lax.broadcasted_iota(I32, (8, groups), 0)).astype(BF16)
    named_mine = dot(mine, named, NT).astype(BF16)
    by_name = dot(named_mine, mask[...].astype(BF16)).astype(BF16)
    by_store = dot(by_name, named).astype(BF16)
    for n in range(16):
        g = lax.broadcasted_iota(I32, (1, keys), 1) // half
        kk, dx = g // 4, g % 4
        store = 2 * (((z + n // 4) % 4) * 16 + ((x + dx) % 4) * 4 + (y + n % 4) % 4) + kk
        pick = (lax.broadcasted_iota(I32, (groups, keys), 0) == store).astype(BF16)
        bias[:, n * keys : (n + 1) * keys] = (1.0 - dot(by_store, pick)) * MASKED

    arrived(kx[0])
    kx2 = {0: kx_relay(0)}
    arrived(kz)
    kz2 = kz_relay()
    kx[1], kx[3] = kx_send(1), kx_send(3)

    loads[0].wait()
    for h in range(heads):
        a = dot(q_nope[:, h * nope : (h + 1) * nope], w_uk[h]).astype(BF16)
        b = q_rope[:, h * rope : (h + 1) * rope]
        for i in range(2):
            r = pl.ds(i * rows + h * half, half)
            Q[r, :latent] = a[i * half : (i + 1) * half]
            Q[r, latent:] = b[i * half : (i + 1) * half]

    arrived(kx2[0])
    ky, ky2, sh = {0: ky_send(0)}, {}, {(0, 0): share(0, 0)}
    arrived(kz2)
    kx[2] = kx_send(2)
    for dz in (1, 3):
        arrived(kx[dz])
        kx2[dz] = kx_relay(dz)
    arrived(wz)
    wz2 = wz_relay()
    arrived([sh[0, 0]])
    attend(0, 0, True)
    for dz in (1, 3):
        arrived(kx2[dz])
        ky[dz] = ky_send(dz)
        sh[dz, 0] = share(dz, 0)
    arrived(kx[2])
    kx2[2] = kx_relay(2)
    wx, wx2 = {0: wx_send(0)}, {}
    arrived(ky[0])
    ky2[0] = ky_relay(0)
    sh[0, 1], sh[0, 3] = share(0, 1), share(0, 3)
    arrived([sh[1, 0]])
    attend(1, 0)
    arrived(kx2[2])
    ky[2] = ky_send(2)
    sh[2, 0] = share(2, 0)
    wx[1], wx[3] = wx_send(1), wx_send(3)
    arrived([sh[3, 0]])
    attend(3, 0)
    arrived([sh[0, 1]])
    attend(0, 1)
    arrived(wz2)
    wx[2] = wx_send(2)
    before = 0
    for dz in (1, 3, 2):
        arrived(ky[dz])
        ky2[dz] = ky_relay(dz)
        sh[dz, 1], sh[dz, 3] = share(dz, 1), share(dz, 3)
        arrived(ky2[before])
        sh[before, 2] = share(before, 2)
        arrived([sh[before, 3]])
        attend(before, 3)
        arrived(wx[before])
        wx2[before] = wx_relay(before)
        arrived([sh[before, 2]])
        attend(before, 2)
        arrived([sh[dz, 1]])
        attend(dz, 1)
        if dz == 1:
            arrived([sh[2, 0]])
            attend(2, 0)
        before = dz
    arrived([sh[2, 3]])
    attend(2, 3)
    arrived(ky2[2])
    sh[2, 2] = share(2, 2)
    arrived(wx[2])
    wx2[2] = wx_relay(2)
    arrived([sh[2, 2]])
    attend(2, 2)

    loads[1].wait()
    inv = 1.0 / jnp.sum(lanes[...], axis=1, keepdims=True)
    for h in range(heads):
        u, v = h * half, rows + h * half
        a = jnp.concatenate([acc[u : u + half, :] * inv[u : u + half], acc[v : v + half, :] * inv[v : v + half]], axis=0)
        H[0, :, h * 128 : (h + 1) * 128] = dot(a.astype(BF16), w_uv[h]).astype(BF16)
    hy = push(H.at[0], H.at[3], dev(dy=1)), push(H.at[0], H.at[1], dev(dy=3))
    arrived(hy)
    hy2 = (push(H.at[3, wl], H.at[2, wl], dev(dy=1)), push(H.at[1, wh], H.at[2, wh], dev(dy=3)))
    for dz in range(4):
        arrived(wx2[dz])
    arrived(hy2)

    depth = heads * w_uv.shape[2]
    hs = H[...].reshape(4 * 64, depth)

    def product(k):
        return dot(hs, W[:, pl.ds(2 * k, 2)].reshape(512, depth), NT)

    XS[...] = product(other).astype(BF16)
    xs = push(XS, XR, sibling)
    kept = product(core)
    arrived([xs])
    total = (kept + XR[...].astype(F32)).astype(BF16)
    for zz in range(4):
        for dy in range(4):
            S[zz, dy] = total[dy * 64 : (dy + 1) * 64, zz * 128 : (zz + 1) * 128]
    last = [push(S.at[(zl + dl) % 4, dy], R.at[dl, dy], dev(dl=dl, dy=dy))
            for dl in (2, 3, 1, 0) for dy in (2, 1, 3, 0) if dl or dy]
    R[0, 0] = S[pl.ds(zl, 1), 0][0]
    arrived(last)
    for dy in range(4):
        a = R[0, dy].astype(F32) + R[1, dy].astype(F32) + R[2, dy].astype(F32) + R[3, dy].astype(F32)
        A[pl.ds((y + 4 - dy) % 4, 1)] = a[None]
    out[...] = jnp.concatenate(
        [A[yy][:, q * 64 : q * 64 + cols] for q in range(2) for yy in range(4)], axis=1
    ).astype(out.dtype)
    for d in pending:
        d.wait_send()


def solution(mesh):
    def on_device(q_nope, q_rope, kv, w_uk, w_uv, w_out, order, mask):
        heads, nope, latent = w_uk.shape
        rows, width = kv.shape
        half, cols = rows // 2, w_out.shape[1]
        vdim = w_uv.shape[2]
        groups = order.shape[0]
        in_vmem = pl.BlockSpec(memory_space=pltpu.VMEM)
        in_hbm = pl.BlockSpec(memory_space=pl.ANY)
        return pl.pallas_call(
            kernel,
            out_shape=jax.ShapeDtypeStruct((rows, 8 * cols), BF16),
            in_specs=[in_vmem, in_vmem, in_vmem, in_hbm, in_hbm, in_vmem, in_vmem, in_vmem],
            out_specs=in_vmem,
            scratch_shapes=[
                pltpu.VMEM((4, 4, 2, 4, half, width), BF16),
                pltpu.VMEM((4, 4, 64, heads * vdim), BF16),
                pltpu.VMEM((heads * rows, width), BF16),
                pltpu.VMEM((heads * rows, latent), F32),
                pltpu.VMEM((heads * rows, 128), F32),
                pltpu.VMEM((8, 64 * rows), F32),
                pltpu.VMEM(w_uk.shape, BF16),
                pltpu.VMEM(w_uv.shape, BF16),
                pltpu.VMEM((4, rows, heads * vdim), BF16),
                pltpu.VMEM((4 * rows, 512), BF16),
                pltpu.VMEM((4 * rows, 512), BF16),
                pltpu.VMEM((4, 4, rows, 128), BF16),
                pltpu.VMEM((4, 4, rows, 128), BF16),
                pltpu.VMEM((4, rows, 128), F32),
                pltpu.SemaphoreType.DMA((N_SEMS,)),
                pltpu.SemaphoreType.DMA((N_SEMS,)),
                pltpu.SemaphoreType.DMA((2,)),
            ],
            compiler_params=pltpu.CompilerParams(
                collective_id=0, has_side_effects=True, vmem_limit_bytes=48 * 1024 * 1024
            ),
        )(q_nope, q_rope, kv, w_uk, w_uv, w_out, order.reshape(1, groups), mask)

    in_specs = (P("ctx", "tp"), P("ctx", "tp"), P("ctx", None), P("tp", None, None), P("tp", None, None),
                P("tp", "ctx"), P(), P())
    return jax.shard_map(on_device, mesh=mesh, in_specs=in_specs, out_specs=P("ctx", "tp"), check_vma=False)
```

time: 403 us -> 89.3 us (0.22)
  waiting for transfers between devices: 361 us -> 0 us
  Pallas kernels: 0 us -> 84.8 us
  matrix products: 19.2 us -> 0 us
  between operations: 13.3 us -> 0.08 us
    all_gather x2 -> x0, waiting for transfers between devices: 324 us -> none  [the longest x1 170 us: on_device(): lax.all_gather(w_out, 'ctx', axis=1, tiled=True)]
    pallas_call x0 -> x1, Pallas kernels: none -> 84.8 us  [on_device(): pl.pallas_call(kernel, out_shape=jax.ShapeDtypeStruct((rows, 8 * cols), B...]
    unnamed x4 -> x0, waiting for transfers between devices: 37 us -> none
    dot_general x16 -> x0, matrix products: 19.2 us -> none  [the longest x4 7.75 us: on_device(): lax.dot_general(queries, key_block, (((1,), (1,)), ((), ())), preferred_e...]
  transfers between devices with their start and end apart: 3 -> 0, of which waited for: 3 -> 0; matrix products, arithmetic and copies ran while one was open for 4% -> 0% of each run, Pallas kernels for 0% -> 0%
where the time goes in v1:
time: 89.3 us; the launch traced here: 89.1 us
  Pallas kernels  84.8 us (95%)
  local copies, waits for them, and re-layouts  4.21 us (5%)
    pallas_call x1, Pallas kernels, on_device(): pl.pallas_call(kernel, out_shape=jax.ShapeDtypeStruct((rows, 8 * cols), B...  84.8 us
    unnamed x16, local copies, waits for them, and re-layouts  4.21 us

profile of v1, /device:TPU:1, one launch (start us, length us, event | category | flops | bytes accessed | tf_op | source)
XLA Modules:
  0.0 89.1 jit_solution(13772538445105742989)
XLA Ops:
  0.0 0.0 copy-start.2
  0.0 0.0 copy-start.3
  0.0 0.0 copy-start.4
  0.0 0.0 copy-start.5
  0.0 0.0 copy-start.6
  0.0 1.1 %copy.9.w_out = bf16[1024,56]{1,0:T(8,128)(2,1)S(1)} copy(bf16[1024,56]{0,1:T(8,128)(2,1)} %param.13) | data formatting | bytes 229376 | tf_op args[5]
  1.1 0.0 copy-done.2
  1.2 0.0 copy-done.3
  1.2 0.0 copy-done.4
  1.2 0.0 copy-done.5
  1.2 0.0 copy-done.6
  1.2 0.0 copy-start
  1.2 1.2 %copy-done = bf16[8,128,512]{2,1,0:T(8,128)(2,1)S(1)} copy-done((bf16[8,128,512]{2,1,0:T(8,128)(2,1)S(1)}, bf16[8,128,512]{2,1,0:T(8,128)(2,1)}, u32[]{:S(2)}) %copy-start) | copy-done | bytes 1048600
  2.4 0.0 copy-start.1
  2.4 1.2 %copy-done.1 = bf16[8,512,128]{2,1,0:T(8,128)(2,1)S(1)} copy-done((bf16[8,512,128]{2,1,0:T(8,128)(2,1)S(1)}, bf16[8,512,128]{2,1,0:T(8,128)(2,1)}, u32[]{:S(2)}) %copy-start.1) | copy-done | bytes 1048600
  3.7 84.8 %shard_map.82 = bf16[64,448]{1,0:T(8,128)(2,1)S(1)} custom-call(bf16[64,1024]{1,0:T(8,128)(2,1)S(1)} %copy-done.2, bf16[64,512]{1,0:T(8,128)(2,1)S(1)} %copy-done.4, bf16[64,576]{1,0:T(8,128)(2,1)S(1)} %copy-done.3, bf16[8,128,512]{2,1,0:T(8,128)(2,1)S(1)} %copy-done, bf16[8,512,128]{2,1,0:T(8,128)(2,1)S(1)} %copy-done.1, bf16[1024,56]{1,0:T(8,128)(2,1)S(1)} %copy.9.w_out, ...), custom_call_target="tpu_custom_call" | custom-call | tf_op jit(solution)/shard_map/pallas_call | solution.py:284
  88.4 0.6 copy.11
Async XLA Ops:
  0.0 1.1 %copy-start.2 = (bf16[64,1024]{1,0:T(8,128)(2,1)S(1)}, bf16[64,1024]{1,0:T(8,128)(2,1)}, u32[]{:S(2)}) copy-start(bf16[64,1024]{1,0:T(8,128)(2,1)} %q_nope.1) | copy-start | bytes 393220
  0.0 1.2 %copy-start.3 = (bf16[64,576]{1,0:T(8,128)(2,1)S(1)}, bf16[64,576]{1,0:T(8,128)(2,1)}, u32[]{:S(2)}) copy-start(bf16[64,576]{1,0:T(8,128)(2,1)} %kv.1) | copy-start | bytes 221188
  0.0 1.2 %copy-start.4 = (bf16[64,512]{1,0:T(8,128)(2,1)S(1)}, bf16[64,512]{1,0:T(8,128)(2,1)}, u32[]{:S(2)}) copy-start(bf16[64,512]{1,0:T(8,128)(2,1)} %q_rope.1) | copy-start | bytes 196612
  0.0 1.2 %copy-start.5 = (s32[128,128]{1,0:T(8,128)S(1)}, s32[128,128]{1,0:T(8,128)}, u32[]{:S(2)}) copy-start(s32[128,128]{1,0:T(8,128)} %mask.1) | copy-start | bytes 196612
  0.0 1.2 %copy-start.6 = (s32[128]{0:T(128)S(1)}, s32[128]{0:T(128)}, u32[]{:S(2)}) copy-start(s32[128]{0:T(128)} %param.14) | copy-start | bytes 1540
  1.2 1.2 %copy-start = (bf16[8,128,512]{2,1,0:T(8,128)(2,1)S(1)}, bf16[8,128,512]{2,1,0:T(8,128)(2,1)}, u32[]{:S(2)}) copy-start(bf16[8,128,512]{2,1,0:T(8,128)(2,1)} %w_uk_hbm.1) | copy-start | bytes 3145732
  2.4 1.2 %copy-start.1 = (bf16[8,512,128]{2,1,0:T(8,128)(2,1)S(1)}, bf16[8,512,128]{2,1,0:T(8,128)(2,1)}, u32[]{:S(2)}) copy-start(bf16[8,512,128]{2,1,0:T(8,128)(2,1)} %w_uv_hbm.1) | copy-start | bytes 3145732

commit v2 on v1

v2 whole, which is shorter than its diff:
```python
import jax
import jax.numpy as jnp
from jax import lax
from jax.experimental import pallas as pl
from jax.experimental.pallas import tpu as pltpu
from jax.sharding import PartitionSpec as P

MESH = pl.DeviceIdType.MESH
NT = (((1,), (1,)), ((), ()))
NN = (((1,), (0,)), ((), ()))
F32, BF16, I32 = jnp.float32, jnp.bfloat16, jnp.int32
MASKED = -1e30
N_SEMS = 128


def dot(a, b, dims=NN):
    return lax.dot_general(a, b, dims, preferred_element_type=F32)


def kernel(q_nope_hbm, q_rope_hbm, kv_hbm, w_uk_hbm, w_uv_hbm, w_out_hbm, order, mask, out,
           K, W, Q, acc, lanes, bias, q_nope, q_rope, w_uk, w_uv, w_own, H, XS, XR, S, R, A, send, recv, local):
    heads, nope, latent = w_uk.shape
    rope = q_rope.shape[1] // heads
    half = q_nope.shape[0] // 2
    rows = heads * half
    cols = w_own.shape[0]
    keys = 8 * half
    scale = (nope + rope) ** -0.5 * 1.4426950408889634

    c, t = lax.axis_index("ctx"), lax.axis_index("tp")
    z, x, y = c // 16, (c // 4) % 4, c % 4
    zl, core = t // 2, t % 2
    other = 1 - core

    def dev(dz=0, dx=0, dy=0, dl=0, k=core):
        cc = ((z + dz) % 4) * 16 + ((x + dx) % 4) * 4 + (y + dy) % 4
        return (cc, ((zl + dl) % 4) * 2 + k)

    sibling = dev(k=other)
    barrier = pltpu.get_barrier_semaphore()
    partners = [dev(dz=1), dev(dz=3), dev(dx=1), dev(dx=2), dev(dx=3), sibling]
    partners += [dev(dl=dl, dy=dy) for dl in range(4) for dy in range(4) if dl or dy]
    for p in partners:
        pl.semaphore_signal(barrier, inc=1, device_id=p, device_id_type=MESH)

    own_rows = kv_hbm.at[pl.ds(pl.multiple_of(core * half, half), half)]
    loads = [
        pltpu.make_async_copy(src, dst, local.at[i])
        for i, (src, dst) in enumerate([
            (own_rows, K.at[0, 0, core, 0]), (w_out_hbm, w_own), (q_nope_hbm, q_nope), (q_rope_hbm, q_rope),
            (w_uk_hbm, w_uk), (w_uv_hbm, w_uv)])
    ]
    for d in loads:
        d.start()

    pending, used = [], [0]

    def push(src, dst, to):
        i = used[0]
        used[0] += 1
        d = pltpu.make_async_remote_copy(src, dst, send.at[i], recv.at[i], device_id=to, device_id_type=MESH)
        d.start()
        pending.append(d)
        return d

    def arrived(ds):
        for d in ds:
            d.wait_recv()

    lo, hi = pl.ds(0, half // 2), pl.ds(half // 2, half // 2)

    def first(dz, a):
        return dev(dx=a) if dz == 0 else dev(dx=a * other, dy=a * core)

    def second(dz, a):
        return dev(dy=a) if dz == 0 else dev(dx=a * core, dy=a * other)

    def kz_send():
        a = K.at[0, 0, core, 0]
        p, q = K.at[3, 0, core, 0], K.at[1, 0, core, 0]
        l1, h2 = push(a.at[lo], p.at[lo], dev(dz=1)), push(a.at[hi], q.at[hi], dev(dz=3))
        h1, l2 = push(a.at[hi], p.at[hi], dev(dz=1)), push(a.at[lo], q.at[lo], dev(dz=3))
        return l1, h2, h1, l2

    def kz_relay():
        return (push(K.at[3, 0, core, 0, lo], K.at[2, 0, core, 0, lo], dev(dz=1)),
                push(K.at[1, 0, core, 0, hi], K.at[2, 0, core, 0, hi], dev(dz=3)))

    def kf_send(dz):
        return [push(K.at[dz, 0, core, 0], K.at[dz, 0, core, 4 - a], first(dz, a)) for a in (2, 1, 3)]

    def kg_send(dz):
        return {4 - a: push(K.at[dz, 0, core], K.at[dz, 4 - a, core], second(dz, a)) for a in (1, 3, 2)}

    def share(dz, s):
        return push(K.at[dz, s, core], K.at[dz, s, core], sibling)

    own_w = W.at[z, x]
    wl, wh = pl.ds(0, 32), pl.ds(32, 32)

    def wz_send():
        l, h = W.at[z, x, wl], W.at[z, x, wh]
        l1, h2 = push(l, l, dev(dz=1)), push(h, h, dev(dz=3))
        h1, l2 = push(h, h, dev(dz=1)), push(l, l, dev(dz=3))
        return l1, h2, h1, l2

    def wz_relay():
        a, b = W.at[(z + 3) % 4, x, wl], W.at[(z + 1) % 4, x, wh]
        return push(a, a, dev(dz=1)), push(b, b, dev(dz=3))

    def wx_send(dz, part=None, to=(1, 3, 2)):
        a = W.at[(z + dz) % 4, x] if part is None else W.at[(z + dz) % 4, x, part]
        return [push(a, a, dev(dx=d)) for d in to]

    def wx_relay(dz):
        zz = (z + dz) % 4
        a, b = W.at[zz, (x + 3) % 4, wl], W.at[zz, (x + 1) % 4, wh]
        return push(a, a, dev(dx=1)), push(b, b, dev(dx=3))

    def attend(dz, s, begin=False):
        kc = K[dz, s].reshape(keys, latent + rope)
        at = (dz * 4 + s) * keys
        for i in range(2):
            r = pl.ds(i * rows, rows)
            p = dot(Q[r, :], kc, NT) * scale + bias[i : i + 1, at : at + keys]
            if begin:
                key = lax.broadcasted_iota(I32, (rows, keys), 1) - i * keys // 2
                row = lax.broadcasted_iota(I32, (rows, keys), 0) % half
                p = jnp.where((key >= 0) & (key < half) & (key > row), MASKED, p)
            w = jnp.exp2(p)
            part = w[:, :128]
            for j in range(128, keys, 128):
                part = part + w[:, j : j + 128]
            added = dot(w.astype(BF16), kc[:, :latent])
            if begin:
                lanes[r, :] = part
                acc[r, :] = added
            else:
                lanes[r, :] += part
                acc[r, :] += added

    groups = order.shape[1]
    named = (lax.broadcasted_iota(I32, (groups, groups), 0) == order[...]).astype(BF16)
    mine = (lax.broadcasted_iota(I32, (8, groups), 1) == 2 * c + lax.broadcasted_iota(I32, (8, groups), 0)).astype(BF16)
    named_mine = dot(mine, named, NT).astype(BF16)
    by_name = dot(named_mine, mask[...].astype(BF16)).astype(BF16)
    by_store = dot(by_name, named).astype(BF16)
    for n in range(16):
        g = lax.broadcasted_iota(I32, (1, keys), 1) // half
        kk, j = g // 4, g % 4
        dz, s = n // 4, n % 4
        dx, dy = (j, s) if dz == 0 else (jnp.where(kk == 0, j, s), jnp.where(kk == 0, s, j))
        store = 2 * (((z + dz) % 4) * 16 + ((x + dx) % 4) * 4 + (y + dy) % 4) + kk
        pick = (lax.broadcasted_iota(I32, (groups, keys), 0) == store).astype(BF16)
        bias[:, n * keys : (n + 1) * keys] = (1.0 - dot(by_store, pick)) * MASKED

    loads[1].wait()
    own = jnp.concatenate([w_own[...], jnp.zeros((64 - cols, w_own.shape[1]), BF16)], axis=0)
    W[pl.ds(z, 1), pl.ds(x, 1)] = own[None, None]

    for d in loads[2:5]:
        d.wait()
    for h in range(heads):
        a = dot(q_nope[:, h * nope : (h + 1) * nope], w_uk[h]).astype(BF16)
        b = q_rope[:, h * rope : (h + 1) * rope]
        for i in range(2):
            r = pl.ds(i * rows + h * half, half)
            Q[r, :latent] = a[i * half : (i + 1) * half]
            Q[r, latent:] = b[i * half : (i + 1) * half]

    loads[0].wait()
    pl.semaphore_wait(barrier, len(partners))

    kz = kz_send()
    kf, kg, sh = {0: kf_send(0)}, {}, {}
    wx = {0: wx_send(0)}

    def pass_on(dz):
        arrived(kf[dz])
        kg[dz] = kg_send(dz)
        sh[dz, 0] = share(dz, 0)

    def hand_over(dz):
        for s in (3, 1, 2):
            arrived([kg[dz][s]])
            sh[dz, s] = share(dz, s)

    def use(dz, s, begin=False):
        arrived([sh[dz, s]])
        attend(dz, s, begin)

    pass_on(0)
    arrived(kz[:2])
    kz2 = kz_relay()
    arrived(kz[2:])
    kf[1], kf[3] = kf_send(1), kf_send(3)
    wz = wz_send()
    use(0, 0, True)
    pass_on(1)
    pass_on(3)
    arrived(kz2)
    kf[2] = kf_send(2)
    hand_over(0)
    use(0, 3)
    use(0, 1)
    pass_on(2)
    use(0, 2)
    use(1, 0)
    use(3, 0)
    arrived(wz[:2])
    wz2 = wz_relay()
    hand_over(1)
    use(2, 0)
    use(1, 3)
    hand_over(3)
    use(1, 1)
    use(1, 2)
    arrived(wz[2:])
    wx[1], wx[3] = wx_send(1, to=(1, 3)), wx_send(3, to=(1, 3))
    use(3, 3)
    hand_over(2)
    use(3, 1)
    use(3, 2)
    use(2, 3)
    use(2, 1)
    arrived(wx[1])
    arrived(wx[3])
    wx[4], wx[5] = wx_relay(1), wx_relay(3)
    use(2, 2)

    loads[5].wait()
    inv = 1.0 / jnp.sum(lanes[...], axis=1, keepdims=True)
    vdim = w_uv.shape[2]
    piece = heads // 2
    hy = []
    for h in range(heads):
        u, v = h * half, rows + h * half
        a = jnp.concatenate([acc[u : u + half, :] * inv[u : u + half], acc[v : v + half, :] * inv[v : v + half]], axis=0)
        at = (h % piece) * vdim
        H[h // piece, 0, :, at : at + vdim] = dot(a.astype(BF16), w_uv[h]).astype(BF16)
        if h % piece == piece - 1:
            g = h // piece
            hy += [push(H.at[g, 0], H.at[g, 4 - d], dev(dy=d)) for d in (2, 1, 3)]
    arrived(wz2)
    wx[2] = wx_send(2)
    for d in wx:
        if d not in (1, 3):
            arrived(wx[d])
    arrived(hy)

    width = piece * vdim

    def product(k):
        w = W[:, pl.ds(2 * k, 2)].reshape(512, 2 * width)
        a, b = H[0].reshape(256, width), H[1].reshape(256, width)
        return dot(a, w[:, :width], NT) + dot(b, w[:, width:], NT)

    XS[...] = product(other).astype(BF16)
    xs = push(XS, XR, sibling)
    kept = product(core)
    arrived([xs])
    total = (kept + XR[...].astype(F32)).astype(BF16)
    for zz in range(4):
        for dy in range(4):
            S[zz, dy] = total[dy * 64 : (dy + 1) * 64, zz * 128 : (zz + 1) * 128]
    last = [push(S.at[(zl + dl) % 4, dy], R.at[dl, dy], dev(dl=dl, dy=dy))
            for dl in (2, 3, 1, 0) for dy in (2, 1, 3, 0) if dl or dy]
    R[0, 0] = S[pl.ds(zl, 1), 0][0]
    arrived(last)
    for dy in range(4):
        a = R[0, dy].astype(F32) + R[1, dy].astype(F32) + R[2, dy].astype(F32) + R[3, dy].astype(F32)
        A[pl.ds((y + 4 - dy) % 4, 1)] = a[None]
    out[...] = jnp.concatenate(
        [A[yy][:, q * 64 : q * 64 + cols] for q in range(2) for yy in range(4)], axis=1
    ).astype(out.dtype)
    for d in pending:
        d.wait_send()


def solution(mesh):
    def on_device(q_nope, q_rope, kv, w_uk, w_uv, w_out, order, mask):
        heads, nope, latent = w_uk.shape
        rows, width = kv.shape
        half, cols = rows // 2, w_out.shape[1]
        vdim = w_uv.shape[2]
        groups = order.shape[0]
        in_vmem = pl.BlockSpec(memory_space=pltpu.VMEM)
        in_hbm = pl.BlockSpec(memory_space=pl.ANY)
        return pl.pallas_call(
            kernel,
            out_shape=jax.ShapeDtypeStruct((rows, 8 * cols), BF16),
            in_specs=[in_hbm] * 6 + [in_vmem] * 2,
            out_specs=in_vmem,
            scratch_shapes=[
                pltpu.VMEM((4, 4, 2, 4, half, width), BF16),
                pltpu.VMEM((4, 4, 64, heads * vdim), BF16),
                pltpu.VMEM((heads * rows, width), BF16),
                pltpu.VMEM((heads * rows, latent), F32),
                pltpu.VMEM((heads * rows, 128), F32),
                pltpu.VMEM((8, 64 * rows), F32),
                pltpu.VMEM(q_nope.shape, BF16),
                pltpu.VMEM(q_rope.shape, BF16),
                pltpu.VMEM(w_uk.shape, BF16),
                pltpu.VMEM(w_uv.shape, BF16),
                pltpu.VMEM((cols, heads * vdim), BF16),
                pltpu.VMEM((2, 4, rows, heads * vdim // 2), BF16),
                pltpu.VMEM((4 * rows, 512), BF16),
                pltpu.VMEM((4 * rows, 512), BF16),
                pltpu.VMEM((4, 4, rows, 128), BF16),
                pltpu.VMEM((4, 4, rows, 128), BF16),
                pltpu.VMEM((4, rows, 128), F32),
                pltpu.SemaphoreType.DMA((N_SEMS,)),
                pltpu.SemaphoreType.DMA((N_SEMS,)),
                pltpu.SemaphoreType.DMA((6,)),
            ],
            compiler_params=pltpu.CompilerParams(
                collective_id=0, has_side_effects=True, vmem_limit_bytes=60 * 1024 * 1024
            ),
        )(q_nope, q_rope, kv, w_uk, w_uv, w_out.T, order.reshape(1, groups), mask)

    in_specs = (P("ctx", "tp"), P("ctx", "tp"), P("ctx", None), P("tp", None, None), P("tp", None, None),
                P("tp", "ctx"), P(), P())
    return jax.shard_map(on_device, mesh=mesh, in_specs=in_specs, out_specs=P("ctx", "tp"), check_vma=False)
```

time: 89.3 us -> 75.4 us (0.84)
  Pallas kernels: 84.8 us -> 73.7 us
  local copies, waits for them, and re-layouts: 4.21 us -> 1.47 us
    pallas_call x1, Pallas kernels: 84.8 us -> 73.7 us  [on_device(): pl.pallas_call(kernel, out_shape=jax.ShapeDtypeStruct((rows, 8 * cols), B...]
    unnamed x16 -> x1, local copies, waits for them, and re-layouts: 4.21 us -> 1.47 us
where the time goes in v2:
time: 75.4 us; the launch traced here: 75.1 us
  Pallas kernels  73.7 us (98%)
  local copies, waits for them, and re-layouts  1.47 us (2%)
    pallas_call x1, Pallas kernels, on_device(): pl.pallas_call(kernel, out_shape=jax.ShapeDtypeStruct((rows, 8 * cols), B...  73.7 us

profile of v2, /device:TPU:1, one launch (start us, length us, event | category | flops | bytes accessed | tf_op | source)
XLA Modules:
  0.0 75.1 jit_solution(5709435198919347899)
XLA Ops:
  0.0 73.7 %shard_map.82 = bf16[64,448]{1,0:T(8,128)(2,1)} custom-call(bf16[64,1024]{1,0:T(8,128)(2,1)} %q_nope_hbm.1, bf16[64,512]{1,0:T(8,128)(2,1)} %q_rope_hbm.1, bf16[64,576]{1,0:T(8,128)(2,1)} %kv_hbm.1, bf16[8,128,512]{2,1,0:T(8,128)(2,1)} %w_uk_hbm.1, bf16[8,512,128]{2,1,0:T(8,128)(2,1)} %w_uv_hbm.1, bf16[56,1024]{1,0:T(8,128)(2,1)} %bitcast.2, ...), custom_call_target="tpu_custom_call" | custom-call | tf_op jit(solution)/shard_map/pallas_call | solution.py:289
  73.7 1.5 %copy.10 = bf16[64,448]{1,0:T(8,128)(2,1)} copy(bf16[64,448]{1,0:T(8,128)(2,1)} %shard_map.82) | data formatting | bytes 114688

commit v3 on v2

--- a/solution.py
+++ b/solution.py
@@ -11,6 +11,8 @@
 F32, BF16, I32 = jnp.float32, jnp.bfloat16, jnp.int32
 MASKED = -1e30
 N_SEMS = 128
+SWAP = (2,)
+RELAY = (0,1,3)
 
 
 def dot(a, b, dims=NN):
@@ -63,6 +65,12 @@
         pending.append(d)
         return d
 
+    done = []
+
+    def sent(d):
+        d.wait_send()
+        done.append(d)
+
     def arrived(ds):
         for d in ds:
             d.wait_recv()
@@ -70,10 +78,10 @@
     lo, hi = pl.ds(0, half // 2), pl.ds(half // 2, half // 2)
 
     def first(dz, a):
-        return dev(dx=a) if dz == 0 else dev(dx=a * other, dy=a * core)
+        return dev(dx=a) if dz not in SWAP else dev(dx=a * other, dy=a * core)
 
     def second(dz, a):
-        return dev(dy=a) if dz == 0 else dev(dx=a * core, dy=a * other)
+        return dev(dy=a) if dz not in SWAP else dev(dx=a * core, dy=a * other)
 
     def kz_send():
         a = K.at[0, 0, core, 0]
@@ -90,7 +98,13 @@
         return [push(K.at[dz, 0, core, 0], K.at[dz, 0, core, 4 - a], first(dz, a)) for a in (2, 1, 3)]
 
     def kg_send(dz):
-        return {4 - a: push(K.at[dz, 0, core], K.at[dz, 4 - a, core], second(dz, a)) for a in (1, 3, 2)}
+        return {4 - a: push(K.at[dz, 0, core], K.at[dz, 4 - a, core], second(dz, a))
+                for a in ((1, 3) if dz in RELAY else (1, 3, 2))}
+
+    def kg_relay(dz):
+        l, h = pl.ds(0, 2), pl.ds(2, 2)
+        return (push(K.at[dz, 3, core, l], K.at[dz, 2, core, l], second(dz, 1)),
+                push(K.at[dz, 1, core, h], K.at[dz, 2, core, h], second(dz, 3)))
 
     def share(dz, s):
         return push(K.at[dz, s, core], K.at[dz, s, core], sibling)
@@ -98,24 +112,22 @@
     own_w = W.at[z, x]
     wl, wh = pl.ds(0, 32), pl.ds(32, 32)
 
-    def wz_send():
-        l, h = W.at[z, x, wl], W.at[z, x, wh]
-        l1, h2 = push(l, l, dev(dz=1)), push(h, h, dev(dz=3))
-        h1, l2 = push(h, h, dev(dz=1)), push(l, l, dev(dz=3))
-        return l1, h2, h1, l2
-
-    def wz_relay():
-        a, b = W.at[(z + 3) % 4, x, wl], W.at[(z + 1) % 4, x, wh]
+    def wz_send(up, down):
+        a, b = W.at[z, x, up], W.at[z, x, down]
         return push(a, a, dev(dz=1)), push(b, b, dev(dz=3))
 
-    def wx_send(dz, part=None, to=(1, 3, 2)):
-        a = W.at[(z + dz) % 4, x] if part is None else W.at[(z + dz) % 4, x, part]
-        return [push(a, a, dev(dx=d)) for d in to]
-
-    def wx_relay(dz):
-        zz = (z + dz) % 4
-        a, b = W.at[zz, (x + 3) % 4, wl], W.at[zz, (x + 1) % 4, wh]
-        return push(a, a, dev(dx=1)), push(b, b, dev(dx=3))
+    def wz_relay(at):
+        a, b = W.at[(z + 3) % 4, x, pl.ds(at, 16)], W.at[(z + 1) % 4, x, pl.ds(32 + at, 16)]
+        return push(a, a, dev(dz=1)), push(b, b, dev(dz=3))
+
+    def wx_send(dz, part, relayed):
+        a = W.at[(z + dz) % 4, x, part]
+        return [push(a, a, dev(dx=d)) for d in ((1, 3) if relayed else (1, 3, 2))]
+
+    def wx_relay(dz, name):
+        d, part = (1, wl) if name == "l" else (3, wh)
+        a = W.at[(z + dz) % 4, (x + 4 - d) % 4, part]
+        return [push(a, a, dev(dx=d))]
 
     def attend(dz, s, begin=False):
         kc = K[dz, s].reshape(keys, latent + rope)
@@ -149,7 +161,7 @@
         g = lax.broadcasted_iota(I32, (1, keys), 1) // half
         kk, j = g // 4, g % 4
         dz, s = n // 4, n % 4
-        dx, dy = (j, s) if dz == 0 else (jnp.where(kk == 0, j, s), jnp.where(kk == 0, s, j))
+        dx, dy = (j, s) if dz not in SWAP else (jnp.where(kk == 0, j, s), jnp.where(kk == 0, s, j))
         store = 2 * (((z + dz) % 4) * 16 + ((x + dx) % 4) * 4 + (y + dy) % 4) + kk
         pick = (lax.broadcasted_iota(I32, (groups, keys), 0) == store).astype(BF16)
         bias[:, n * keys : (n + 1) * keys] = (1.0 - dot(by_store, pick)) * MASKED
@@ -172,8 +184,20 @@
     pl.semaphore_wait(barrier, len(partners))
 
     kz = kz_send()
-    kf, kg, sh = {0: kf_send(0)}, {}, {}
-    wx = {0: wx_send(0)}
+    kf, kg, kg2, sh = {0: kf_send(0)}, {}, {}, {}
+    wz = []
+    wx, wx2 = {}, {}
+
+    def wx_go(dz, name, relayed=True):
+        wx[dz, name] = wx_send(dz, halves[name], relayed)
+
+    def wx_on(dz, name):
+        arrived(wx[dz, name])
+        wx2[dz, name] = wx_relay(dz, name)
+
+    halves = {"l": wl, "h": wh, "a": pl.ds(0, 16), "b": pl.ds(16, 16), "c": pl.ds(32, 16), "d": pl.ds(48, 16)}
+    wx_go(0, "l")
+    wx_go(0, "h")
 
     def pass_on(dz):
         arrived(kf[dz])
@@ -181,51 +205,76 @@
         sh[dz, 0] = share(dz, 0)
 
     def hand_over(dz):
-        for s in (3, 1, 2):
-            arrived([kg[dz][s]])
+        if dz in RELAY:
+            arrived([kg[dz][3], kg[dz][1]])
+            kg2[dz] = kg_relay(dz)
+        for s in (3, 1):
+            arrived([] if dz in RELAY else [kg[dz][s]])
             sh[dz, s] = share(dz, s)
+
+    def hand_over_far(dz):
+        arrived(kg2[dz] if dz in RELAY else [kg[dz][2]])
+        sh[dz, 2] = share(dz, 2)
 
     def use(dz, s, begin=False):
         arrived([sh[dz, s]])
         attend(dz, s, begin)
 
     pass_on(0)
+    wz.append(wz_send(wl, wh))
     arrived(kz[:2])
     kz2 = kz_relay()
     arrived(kz[2:])
     kf[1], kf[3] = kf_send(1), kf_send(3)
-    wz = wz_send()
     use(0, 0, True)
+    hand_over(0)
+    wx_on(0, "l")
+    wx_on(0, "h")
     pass_on(1)
     pass_on(3)
     arrived(kz2)
     kf[2] = kf_send(2)
-    hand_over(0)
+    wz.append(wz_send(wh, wl))
+    hand_over_far(0)
+    arrived(wz[0])
+    wz2 = [wz_relay(0)]
+    wx_go(3, "l")
+    wx_go(1, "h")
     use(0, 3)
     use(0, 1)
     pass_on(2)
+    hand_over(1)
+    hand_over(3)
+    wz2.append(wz_relay(16))
     use(0, 2)
+    arrived(wz[1])
+    wx_go(3, "h")
+    wx_go(1, "l")
     use(1, 0)
     use(3, 0)
-    arrived(wz[:2])
-    wz2 = wz_relay()
-    hand_over(1)
+    wx_on(3, "l")
+    wx_on(1, "h")
+    hand_over_far(1)
+    hand_over_far(3)
+    use(1, 3)
     use(2, 0)
-    use(1, 3)
-    hand_over(3)
     use(1, 1)
+    hand_over(2)
+    arrived(wz2[0])
+    wx_go(2, "a", False)
+    wx_go(2, "c", False)
+    use(3, 3)
+    use(3, 1)
+    hand_over_far(2)
     use(1, 2)
-    arrived(wz[2:])
-    wx[1], wx[3] = wx_send(1, to=(1, 3)), wx_send(3, to=(1, 3))
-    use(3, 3)
-    hand_over(2)
-    use(3, 1)
+    wx_on(3, "h")
+    wx_on(1, "l")
     use(3, 2)
     use(2, 3)
+    arrived(wz2[1])
+    wx_go(2, "b", False)
+    wx_go(2, "d", False)
     use(2, 1)
-    arrived(wx[1])
-    arrived(wx[3])
-    wx[4], wx[5] = wx_relay(1), wx_relay(3)
     use(2, 2)
 
     loads[5].wait()
@@ -241,11 +290,10 @@
         if h % piece == piece - 1:
             g = h // piece
             hy += [push(H.at[g, 0], H.at[g, 4 - d], dev(dy=d)) for d in (2, 1, 3)]
-    arrived(wz2)
-    wx[2] = wx_send(2)
-    for d in wx:
-        if d not in (1, 3):
-            arrived(wx[d])
+    for name in "acbd":
+        arrived(wx[2, name])
+    for d in wx2:
+        arrived(wx2[d])
     arrived(hy)
 
     width = piece * vdim
@@ -274,7 +322,8 @@
         [A[yy][:, q * 64 : q * 64 + cols] for q in range(2) for yy in range(4)], axis=1
     ).astype(out.dtype)
     for d in pending:
-        d.wait_send()
+        if not any(d is e for e in done):
+            d.wait_send()
 
 
 def solution(mesh):

time: 75.4 us -> 71.8 us (0.952)
  Pallas kernels: 73.7 us -> 70.1 us
    pallas_call x1, Pallas kernels: 73.7 us -> 70.1 us  [on_device(): pl.pallas_call(kernel, out_shape=jax.ShapeDtypeStruct((rows, 8 * cols), B...]
where the time goes in v3:
time: 71.8 us; the launch traced here: 71.6 us
  Pallas kernels  70.1 us (98%)
  local copies, waits for them, and re-layouts  1.47 us (2%)
    pallas_call x1, Pallas kernels, on_device(): pl.pallas_call(kernel, out_shape=jax.ShapeDtypeStruct((rows, 8 * cols), B...  70.1 us
    unnamed x1, local copies, waits for them, and re-layouts  1.47 us

profile of v3, /device:TPU:1, one launch (start us, length us, event | category | flops | bytes accessed | tf_op | source)
XLA Modules:
  0.0 71.6 jit_solution(2755177085868877854)
XLA Ops:
  0.0 70.1 %shard_map.82 = bf16[64,448]{1,0:T(8,128)(2,1)} custom-call(bf16[64,1024]{1,0:T(8,128)(2,1)} %q_nope_hbm.1, bf16[64,512]{1,0:T(8,128)(2,1)} %q_rope_hbm.1, bf16[64,576]{1,0:T(8,128)(2,1)} %kv_hbm.1, bf16[8,128,512]{2,1,0:T(8,128)(2,1)} %w_uk_hbm.1, bf16[8,512,128]{2,1,0:T(8,128)(2,1)} %w_uv_hbm.1, bf16[56,1024]{1,0:T(8,128)(2,1)} %bitcast.2, ...), custom_call_target="tpu_custom_call" | custom-call | tf_op jit(solution)/shard_map/pallas_call | solution.py:338
  70.1 1.5 %copy.10 = bf16[64,448]{1,0:T(8,128)(2,1)} copy(bf16[64,448]{1,0:T(8,128)(2,1)} %shard_map.82) | data formatting | bytes 114688

commit v4 on v3

--- a/solution.py
+++ b/solution.py
@@ -289,30 +289,36 @@
         H[h // piece, 0, :, at : at + vdim] = dot(a.astype(BF16), w_uv[h]).astype(BF16)
         if h % piece == piece - 1:
             g = h // piece
-            hy += [push(H.at[g, 0], H.at[g, 4 - d], dev(dy=d)) for d in (2, 1, 3)]
+            hy += [push(H.at[g, 0], H.at[g, 4 - d], dev(dy=d)) for d in (1, 3, 2)]
     for name in "acbd":
         arrived(wx[2, name])
     for d in wx2:
         arrived(wx2[d])
-    arrived(hy)
-
-    width = piece * vdim
-
-    def product(k):
-        w = W[:, pl.ds(2 * k, 2)].reshape(512, 2 * width)
-        a, b = H[0].reshape(256, width), H[1].reshape(256, width)
-        return dot(a, w[:, :width], NT) + dot(b, w[:, width:], NT)
-
-    XS[...] = product(other).astype(BF16)
-    xs = push(XS, XR, sibling)
-    kept = product(core)
-    arrived([xs])
-    total = (kept + XR[...].astype(F32)).astype(BF16)
-    for zz in range(4):
-        for dy in range(4):
-            S[zz, dy] = total[dy * 64 : (dy + 1) * 64, zz * 128 : (zz + 1) * 128]
-    last = [push(S.at[(zl + dl) % 4, dy], R.at[dl, dy], dev(dl=dl, dy=dy))
-            for dl in (2, 3, 1, 0) for dy in (2, 1, 3, 0) if dl or dy]
+    hy = {(i // 3, (3, 1, 2)[i % 3]): d for i, d in enumerate(hy)}
+    arrived([hy[g, d] for g in range(2) for d in (1, 3)])
+
+    deep = W.shape[3] // 2
+
+    def product(k, at):
+        w = W[:, pl.ds(2 * k, 2)].reshape(512, 2 * deep)
+        a, b = (H[g, at : at + 2].reshape(128, deep) for g in range(2))
+        return dot(a, w[:, :deep], NT) + dot(b, w[:, deep:], NT)
+
+    last = []
+    for at in (0, 2):
+        if at:
+            arrived([hy[g, 2] for g in range(2)])
+        r = pl.ds(at * 64, 128)
+        XS[r, :] = product(other, at).astype(BF16)
+        xs = push(XS.at[r], XR.at[r], sibling)
+        kept = product(core, at)
+        arrived([xs])
+        total = (kept + XR[r, :].astype(F32)).astype(BF16)
+        for zz in range(4):
+            for i in range(2):
+                S[zz, at + i] = total[i * 64 : (i + 1) * 64, zz * 128 : (zz + 1) * 128]
+        last += [push(S.at[(zl + dl) % 4, dy], R.at[dl, dy], dev(dl=dl, dy=dy))
+                 for dl in (2, 3, 1, 0) for dy in (at, at + 1) if dl or dy]
     R[0, 0] = S[pl.ds(zl, 1), 0][0]
     arrived(last)
     for dy in range(4):

time: 71.8 us -> 70.9 us (0.987)
  Pallas kernels: 70.1 us -> 69.1 us
    pallas_call x1, Pallas kernels: 70.1 us -> 69.1 us  [on_device(): pl.pallas_call(kernel, out_shape=jax.ShapeDtypeStruct((rows, 8 * cols), B...]
where the time goes in v4:
time: 70.9 us; the launch traced here: 70.6 us
  Pallas kernels  69.1 us (97%)
  local copies, waits for them, and re-layouts  1.47 us (2%)
    pallas_call x1, Pallas kernels, on_device(): pl.pallas_call(kernel, out_shape=jax.ShapeDtypeStruct((rows, 8 * cols), B...  69.1 us
    unnamed x1, local copies, waits for them, and re-layouts  1.47 us

profile of v4, /device:TPU:1, one launch (start us, length us, event | category | flops | bytes accessed | tf_op | source)
XLA Modules:
  0.0 70.6 jit_solution(9303309504901441016)
XLA Ops:
  0.0 69.1 %shard_map.82 = bf16[64,448]{1,0:T(8,128)(2,1)} custom-call(bf16[64,1024]{1,0:T(8,128)(2,1)} %q_nope_hbm.1, bf16[64,512]{1,0:T(8,128)(2,1)} %q_rope_hbm.1, bf16[64,576]{1,0:T(8,128)(2,1)} %kv_hbm.1, bf16[8,128,512]{2,1,0:T(8,128)(2,1)} %w_uk_hbm.1, bf16[8,512,128]{2,1,0:T(8,128)(2,1)} %w_uv_hbm.1, bf16[56,1024]{1,0:T(8,128)(2,1)} %bitcast.2, ...), custom_call_target="tpu_custom_call" | custom-call | tf_op jit(solution)/shard_map/pallas_call | solution.py:344
  69.1 1.5 %copy.10 = bf16[64,448]{1,0:T(8,128)(2,1)} copy(bf16[64,448]{1,0:T(8,128)(2,1)} %shard_map.82) | data formatting | bytes 114688

commit v5 on v4

--- a/solution.py
+++ b/solution.py
@@ -11,7 +11,7 @@
 F32, BF16, I32 = jnp.float32, jnp.bfloat16, jnp.int32
 MASKED = -1e30
 N_SEMS = 128
-SWAP = (2,)
+SWAP = (1, 2)
 RELAY = (0,1,3)
 
 

time: 70.9 us -> 71 us (level)
  no operation moved by 1% of the time
where the time goes in v5:
time: 71 us; the launch traced here: 70.8 us
  Pallas kernels  69.3 us (98%)
  local copies, waits for them, and re-layouts  1.47 us (2%)
    pallas_call x1, Pallas kernels, on_device(): pl.pallas_call(kernel, out_shape=jax.ShapeDtypeStruct((rows, 8 * cols), B...  69.3 us
    unnamed x1, local copies, waits for them, and re-layouts  1.47 us

profile of v5, /device:TPU:1, one launch (start us, length us, event | category | flops | bytes accessed | tf_op | source)
XLA Modules:
  0.0 70.8 jit_solution(11603083024876688656)
XLA Ops:
  0.0 69.3 %shard_map.82 = bf16[64,448]{1,0:T(8,128)(2,1)} custom-call(bf16[64,1024]{1,0:T(8,128)(2,1)} %q_nope_hbm.1, bf16[64,512]{1,0:T(8,128)(2,1)} %q_rope_hbm.1, bf16[64,576]{1,0:T(8,128)(2,1)} %kv_hbm.1, bf16[8,128,512]{2,1,0:T(8,128)(2,1)} %w_uk_hbm.1, bf16[8,512,128]{2,1,0:T(8,128)(2,1)} %w_uv_hbm.1, bf16[56,1024]{1,0:T(8,128)(2,1)} %bitcast.2, ...), custom_call_target="tpu_custom_call" | custom-call | tf_op jit(solution)/shard_map/pallas_call | solution.py:344
  69.3 1.5 %copy.10 = bf16[64,448]{1,0:T(8,128)(2,1)} copy(bf16[64,448]{1,0:T(8,128)(2,1)} %shard_map.82) | data formatting | bytes 114688
